TPU v7x, 256 devices: a whole 4x4x8 slice. The times are simulated.
256 devices in a mesh: dp: 16 (over x_hi, z), tm: 16 (over x_lo, y, core).
Axes of the slice: x: 4 (x_hi: 2, x_lo: 2; x = x_hi * 2 + x_lo), y: 4, z: 8, core: 2. Of those that a mesh axis runs over, the one named last changes fastest.
Arguments:
- tokens: bfloat16 [16, 256, 48, 1152], P('dp', 'tm'), may hold values from -6 to 6
- mod_scale: float32 [16, 1152], P('dp'), may hold values from -0.5 to 0.5
- mod_gate: float32 [16, 1152], P('dp'), may hold values from 0.3 to 3
- w_qkv: bfloat16 [1152, 1728], P('tm'), may hold values from -3 to 3
- w_out: bfloat16 [1152, 576], P('tm'), may hold values from -0.25 to 0.25
- d_out: bfloat16 [16, 256, 48, 1152], P('dp', 'tm'), may hold values from -6 to 6
Outputs:
- d_tokens: bfloat16 [16, 256, 48, 1152], P('dp', 'tm')
- d_w_qkv: float32 [1152, 1728], P('tm', 'dp')
- d_w_out: float32 [1152, 576], P('tm', 'dp')
All inputs are finite; a program needn't handle non-finite values.
Results may differ from a plain program's by a relative error of at most 0.011.
Values may be sent and summed in bfloat16 or wider, within the bound.
A program may use at most 128 MiB of HBM per device.

v0:
```python
import math

import jax
import jax.numpy as jnp
from jax import lax
from jax.sharding import PartitionSpec as P

HEADS = 8


EPS = 1e-06


def mixing(form, left, right):
    return jnp.einsum(form, left, right, preferred_element_type=jnp.float32)


def normalize_rows(rows, scale_vec):
    values = rows.astype(jnp.float32)
    centered = values - jnp.mean(values, axis=-1, keepdims=True)
    inverse_std = lax.rsqrt(jnp.mean(centered * centered, axis=-1, keepdims=True) + EPS)
    unit_rows = centered * inverse_std
    modulated = (unit_rows * (1.0 + scale_vec)).astype(jnp.bfloat16)
    return (modulated, unit_rows, inverse_std)


def attention_grads(projected, attn_grad, head_count):
    frames, patches, width = projected.shape
    head_dim = width // (3 * head_count)
    split_view = projected.reshape(frames, patches, 3, head_count, head_dim)
    queries = split_view[:, :, 0]
    keys_all = split_view[:, :, 1]
    values_all = split_view[:, :, 2]
    factor = 1.0 / math.sqrt(head_dim)
    grad_view = attn_grad.reshape(frames, patches, head_count, head_dim)
    scores = mixing("fphd,gphd->phfg", queries, keys_all) * factor
    highest = jnp.max(scores, axis=-1, keepdims=True)
    expo = jnp.exp(scores - highest)
    probs = expo / jnp.sum(expo, axis=-1, keepdims=True)
    probs_low = probs.astype(jnp.bfloat16)
    attended = mixing("phfg,gphd->fphd", probs_low, values_all).astype(jnp.bfloat16)
    prob_grad = mixing("fphd,gphd->phfg", grad_view, values_all)
    value_grad = mixing("phfg,fphd->gphd", probs_low, grad_view).astype(jnp.bfloat16)
    score_grad = (probs * (prob_grad - jnp.sum(probs * prob_grad, axis=-1, keepdims=True))).astype(
        jnp.bfloat16
    )
    query_grad = (mixing("phfg,gphd->fphd", score_grad, keys_all) * factor).astype(jnp.bfloat16)
    key_grad = (mixing("phfg,fphd->gphd", score_grad, queries) * factor).astype(jnp.bfloat16)
    stacked = jnp.stack([query_grad, key_grad, value_grad], axis=2).reshape(frames, patches, width)
    return (attended.reshape(frames, patches, head_count * head_dim), stacked)


def input_grad(proj_grad, full_qkv, unit_rows, inverse_std, scale_vec, d_rows):
    mod_grad = mixing("fpc,dc->fpd", proj_grad, full_qkv)
    unit_grad = mod_grad * (1.0 + scale_vec)
    branch = inverse_std * (
        unit_grad
        - jnp.mean(unit_grad, axis=-1, keepdims=True)
        - unit_rows * jnp.mean(unit_grad * unit_rows, axis=-1, keepdims=True)
    )
    return (d_rows.astype(jnp.float32) + branch).astype(jnp.bfloat16)


def shards(tokens, mod_scale, mod_gate, w_qkv, w_out, d_out):
    scale_vec = mod_scale[0]
    gate_vec = mod_gate[0]
    full_qkv, full_out = (
        lax.all_gather(w_qkv, "tm", axis=0, tiled=True),
        lax.all_gather(w_out, "tm", axis=0, tiled=True),
    )
    rows = tokens[0]
    d_rows = d_out[0]
    modulated, unit_rows, inverse_std = normalize_rows(rows, scale_vec)
    projected = mixing("fpd,dc->fpc", modulated, full_qkv).astype(jnp.bfloat16)
    branch_grad = (d_rows.astype(jnp.float32) * gate_vec).astype(jnp.bfloat16)
    attn_grad = mixing("fpd,dc->fpc", branch_grad, full_out).astype(jnp.bfloat16)
    proj_patches, grad_patches = (
        lax.all_to_all(projected, "tm", split_axis=1, concat_axis=0, tiled=True),
        lax.all_to_all(attn_grad, "tm", split_axis=1, concat_axis=0, tiled=True),
    )
    attended_patches, proj_grad_patches = attention_grads(proj_patches, grad_patches, HEADS)
    attended, proj_grad = (
        lax.all_to_all(attended_patches, "tm", split_axis=0, concat_axis=1, tiled=True),
        lax.all_to_all(proj_grad_patches, "tm", split_axis=0, concat_axis=1, tiled=True),
    )
    d_rows_out = input_grad(proj_grad, full_qkv, unit_rows, inverse_std, scale_vec, d_rows)
    grad_qkv = mixing("fpd,fpc->dc", modulated, proj_grad)
    grad_out = mixing("fpd,fpc->dc", branch_grad, attended)
    d_tokens = d_rows_out[None]
    part_qkv, part_out = (
        lax.psum_scatter(grad_qkv, "tm", scatter_dimension=0, tiled=True),
        lax.psum_scatter(grad_out, "tm", scatter_dimension=0, tiled=True),
    )
    summed_qkv, summed_out = (
        lax.psum_scatter(part_qkv, "dp", scatter_dimension=1, tiled=True),
        lax.psum_scatter(part_out, "dp", scatter_dimension=1, tiled=True),
    )
    row_total = lax.axis_size("dp") * lax.axis_size("tm") * tokens.shape[1] * tokens.shape[2]
    grad_scale = 1.0 / math.sqrt(row_total)
    return (d_tokens, summed_qkv * grad_scale, summed_out * grad_scale)


def solution(mesh):
    return jax.shard_map(
        shards,
        mesh=mesh,
        in_specs=(
            P("dp", "tm", None, None),
            P("dp", None),
            P("dp", None),
            P("tm", None),
            P("tm", None),
            P("dp", "tm", None, None),
        ),
        out_specs=(P("dp", "tm", None, None), P("tm", "dp"), P("tm", "dp")),
        check_vma=False,
    )
```

profile of v0, /device:TPU:1, one launch (start us, length us, event | category | flops | bytes accessed | tf_op | source)
XLA Modules:
  0.0 530.1 jit_solution(14155515508182081486)
XLA Ops:
  14.0 35.7 %all-gather.5.cloned.1.call-done = bf16[1152,576]{1,0:T(8,128)(2,1)} async-done(((bf16[72,576]{1,0:T(8,128)(2,1)}), bf16[1152,576]{1,0:T(8,128)(2,1)}) %all-gather.5.cloned.1.call-update) | async-done | bytes 1327120 | tf_op jit(solution)/shard_map/all_gather | solution.py:69
  49.7 3.0 fusion.57
  53.9 4.3 all-to-all-start.1
  58.2 39.7 %all-gather.3.cloned.1.call-done = bf16[1152,1728]{1,0:T(8,128)(2,1)} async-done(((bf16[72,1728]{1,0:T(8,128)(2,1)}), bf16[1152,1728]{1,0:T(8,128)(2,1)}) %all-gather.3.cloned.1.call-update) | async-done | bytes 3981328 | tf_op jit(solution)/shard_map/all_gather | solution.py:68
  97.8 6.3 %fusion.30 = bf16[16,48,1728]{2,1,0:T(8,128)(2,1)S(1)} fusion(bf16[1152,1728]{1,0:T(8,128)(2,1)} %all-gather.3.cloned.1.call-done, bf16[1,16,48,1152]{3,2,1,0:T(8,128)(2,1)S(1)} %copy-done.1, f32[1152]{0:T(1024)S(1)} %add_reduce_fusion, f32[16,48]{1,0:T(8,128)S(1)} %add_rsqrt_fusion, f32[16,48]{1,0:T(8,128)S(1)} %broadcast_multiply_fusion.2), kind=kOutput, calls=%fused_computation.37 | convolution fusion | flops 3063398400 | bytes 8415744 | tf_op jit(solution)/shard_map/fpd,dc->fpc/dot_general | solution.py:15
  107.5 3.8 all-to-all-start
  113.5 3.8 reshape.57
  120.1 26.4 %all-to-all-done = bf16[16,48,1728]{2,0,1:T(8,128)(2,1)S(1)} async-done(((bf16[16,48,1728]{2,0,1:T(8,128)(2,1)}), bf16[16,48,1728]{2,0,1:T(8,128)(2,1)S(1)}, u32[]{:S(2)}, u32[]{:S(2)}) %all-to-all-start) | async-done | bytes 2654240 | tf_op jit(solution)/shard_map/all_to_all | solution.py:78
  150.0 6.2 %reshape.56 = bf16[256,3,3,8,72]{4,3,2,0,1:T(8,128)(2,1)} reshape(bf16[16,16,3,1728]{3,1,0,2:T(8,128)(2,1)S(1)} %copy.39) | data formatting | bytes 5308416 | tf_op jit(solution)/shard_map/reshape | solution.py:30
  156.2 3.8 fusion.84
  165.7 4.8 fusion.85
  175.4 9.0 %all-to-all-start.3 = ((bf16[256,3,576]{2,1,0:T(4,128)(2,1)}), bf16[256,3,576]{2,1,0:T(4,128)(2,1)}, u32[]{:S(2)}, u32[]{:S(2)}) async-start(bf16[256,3,576]{2,1,0:T(4,128)(2,1)} %copy.57), calls=%async_computation.4 | async-start | bytes 2621440 | tf_op jit(solution)/shard_map/all_to_all | solution.py:83
  184.4 3.9 multiply_reduce_fusion
  188.3 4.4 multiply_convert_fusion
  194.8 8.4 %all-to-all-done.3 = bf16[256,3,576]{2,1,0:T(4,128)(2,1)} async-done(((bf16[256,3,576]{2,1,0:T(4,128)(2,1)}), bf16[256,3,576]{2,1,0:T(4,128)(2,1)}, u32[]{:S(2)}, u32[]{:S(2)}) %all-to-all-start.3) | async-done | bytes 884768 | tf_op jit(solution)/shard_map/all_to_all | solution.py:83
  205.0 3.2 convolution_bitcast_fusion.1
  210.3 3.9 fusion.68
  214.7 4.9 copy.51
  219.6 56.7 %all_to_all.66 = bf16[256,3,1728]{2,1,0:T(4,128)(2,1)S(1)} all-to-all(bf16[256,3,1728]{2,1,0:T(4,128)(2,1)} %copy.51), channel_id=1, replica_groups=mesh['dp'=16,'tm'=16] {'tm'}, dimensions={0} | all-to-all | bytes 5308416 | tf_op jit(solution)/shard_map/all_to_all | solution.py:84
  278.9 6.6 %convolution_bitcast_fusion = f32[1152,1728]{1,0:T(8,128)} fusion(bf16[16,48,1728]{2,0,1:T(8,128)(2,1)S(1)} %bitcast.142, bf16[1,16,48,1152]{3,2,1,0:T(8,128)(2,1)S(1)} %copy-done.2, f32[1152]{0:T(1024)S(1)} %add_reduce_fusion, f32[16,48]{1,0:T(8,128)S(1)} %add_rsqrt_fusion, f32[16,48]{1,0:T(8,128)S(1)} %broadcast_multiply_fusion.2), kind=kOutput, calls=%fused_computation.1 | convolution fusion | flops 3062071296 | bytes 12397056 | tf_op jit(solution)/shard_map/fpd,fpc->dc/dot_general | solution.py:15
  288.1 9.3 %fusion.83 = (f32[16,48]{1,0:T(8,128)S(1)}, f32[16,48]{1,0:T(8,128)S(1)}, f32[16,48,1152]{2,1,0:T(8,128)}) fusion(f32[16,48]{1,0:T(8,128)S(1)} %add_rsqrt_fusion, f32[16,48]{1,0:T(8,128)S(1)} %broadcast_multiply_fusion.2, bf16[1,16,48,1152]{3,2,1,0:T(8,128)(2,1)S(1)} %copy-done.2, f32[1152]{0:T(1024)} %copy-done.16, ...), kind=kOutput, calls=%fused_computation.85 | convolution fusion | flops 3063839232 | bytes 11960832 | tf_op jit(solution)/shard_map/fpc,dc->fpd/dot_general | solution.py:15
  298.0 70.7 %reduce-scatter.8.cloned.1.call-done = f32[72,1728]{1,0:T(8,128)} async-done(((f32[1152,1728]{1,0:T(8,128)}), f32[72,1728]{1,0:T(8,128)}) %reduce-scatter.8.cloned.1.call-update) | async-done | bytes 497680 | tf_op jit(solution)/shard_map/reduce_scatter | solution.py:91
  368.8 3.8 fusion.41
  372.5 147.8 %all-reduce.6.cloned.1.call-done = (f32[72,1728]{1,0:T(8,128)}, f32[72,576]{1,0:T(8,128)}) async-done(((f32[72,1728]{1,0:T(8,128)}, f32[72,576]{1,0:T(8,128)}), (f32[72,1728]{1,0:T(8,128)}, f32[72,576]{1,0:T(8,128)})) %all-reduce.6.cloned.1.call-update) | async-done | bytes 663568
  (78 shorter events, 44.3 us)
Async XLA Ops:
  7.2 42.6 %copy-start.10 = (bf16[1,16,48,1152]{3,2,1,0:T(8,128)(2,1)S(1)}, bf16[1,16,48,1152]{3,2,1,0:T(8,128)(2,1)}, u32[]{:S(2)}) copy-start(bf16[1,16,48,1152]{3,2,1,0:T(8,128)(2,1)} %param.11) | copy-start | bytes 5308420
  7.2 42.6 %all-gather.5.cloned.1.call-start = ((), (), s32[]{:S(2)}) async-start(), calls=%async_computation.7 | async-start | bytes 1566720 | tf_op jit(solution)/shard_map/all_gather | solution.py:69
  7.9 89.9 %all-gather.3.cloned.1.call-start = ((), (), s32[]{:S(2)}) async-start(), calls=%async_computation.6 | async-start | bytes 4386816 | tf_op jit(solution)/shard_map/all_gather | solution.py:68
  10.1 266.7 %copy-start.16 = (f32[1152]{0:T(1024)}, f32[1152]{0:T(1024)S(1)}, u32[]{:S(2)}) copy-start(f32[1152]{0:T(1024)S(1)} %add_reduce_fusion) | copy-start | bytes 13828
  52.8 45.1 %copy-start.1 = (bf16[1,16,48,1152]{3,2,1,0:T(8,128)(2,1)S(1)}, bf16[1,16,48,1152]{3,2,1,0:T(8,128)(2,1)}, u32[]{:S(2)}) copy-start(bf16[1,16,48,1152]{3,2,1,0:T(8,128)(2,1)} %param.6) | copy-start | bytes 5308420
  53.9 52.6 %all-to-all-start.1 = ((bf16[16,48,576]{2,0,1:T(8,128)(2,1)}), bf16[16,48,576]{2,0,1:T(8,128)(2,1)S(1)}, u32[]{:S(2)}, u32[]{:S(2)}) async-start(bf16[16,48,576]{2,0,1:T(8,128)(2,1)} %copy.42), calls=%async_computation.1 | async-start | bytes 1966080 | tf_op jit(solution)/shard_map/all_to_all | solution.py:79
  107.5 39.0 %all-to-all-start = ((bf16[16,48,1728]{2,0,1:T(8,128)(2,1)}), bf16[16,48,1728]{2,0,1:T(8,128)(2,1)S(1)}, u32[]{:S(2)}, u32[]{:S(2)}) async-start(bf16[16,48,1728]{2,0,1:T(8,128)(2,1)} %copy.38), calls=%async_computation | async-start | bytes 5505024 | tf_op jit(solution)/shard_map/all_to_all | solution.py:78
  146.4 1.5 copy-start.3
  163.6 2.1 copy-start.5
  164.6 1.1 copy-start.4
  165.7 4.8 copy-start.15
  170.5 2.7 copy-start
  173.2 11.2 %copy-start.13 = (bf16[256,3,8,72]{0,3,2,1:T(8,128)(2,1)S(1)}, bf16[256,3,8,72]{0,3,2,1:T(8,128)(2,1)}, u32[]{:S(2)}) copy-start(bf16[256,3,8,72]{0,3,2,1:T(8,128)(2,1)} %copy.45) | copy-start | bytes 2654212
  175.4 27.8 %all-to-all-start.3 = ((bf16[256,3,576]{2,1,0:T(4,128)(2,1)}), bf16[256,3,576]{2,1,0:T(4,128)(2,1)}, u32[]{:S(2)}, u32[]{:S(2)}) async-start(bf16[256,3,576]{2,1,0:T(4,128)(2,1)} %copy.57), calls=%async_computation.4 | async-start | bytes 2621440 | tf_op jit(solution)/shard_map/all_to_all | solution.py:83
  184.4 113.7 %reduce-scatter.10.cloned.1.call-start = ((), (), s32[]{:S(2)}) async-start(), calls=%async_computation.9 | async-start | bytes 3133440
  188.3 4.4 copy-start.6
  203.2 1.9 copy-start.11
  208.3 160.5 %reduce-scatter.8.cloned.1.call-start = ((), (), s32[]{:S(2)}) async-start(), calls=%async_computation.8 | async-start | bytes 8773632 | tf_op jit(solution)/shard_map/reduce_scatter | solution.py:91
  208.3 1.9 copy-start.14
  210.2 4.0 copy-start.8
  276.6 2.3 copy-start.2
  276.8 1.5 copy-start.9
  285.6 234.7 %all-reduce.6.cloned.1.call-start = ((), (), s32[]{:S(2)}) async-start(), calls=%async_computation.10 | async-start | bytes 1400832
  288.1 80.6 %copy-start.12 = (bf16[1,16,48,1152]{3,2,1,0:T(8,128)(2,1)S(1)}, bf16[1,16,48,1152]{3,2,1,0:T(8,128)(2,1)}, u32[]{:S(2)}) copy-start(bf16[1,16,48,1152]{3,2,1,0:T(8,128)(2,1)} %param.11) | copy-start | bytes 5308420
  (2 other events, 1.6 us)
Sparse Core Ops, SparseCore 0:
  9.9 39.8 all-gather.4
  51.6 46.2 all-gather.2
  208.4 82.3 reduce-scatter.9
  293.2 75.4 reduce-scatter.7
  371.5 148.7 all-reduce.5
where the time goes:
time: 541 us; the launch traced here: 530 us
  waiting for transfers between devices  330 us (61%)
  blocking collectives  56.7 us (10%)
  local copies, waits for them, and re-layouts  46.7 us (9%)
  matrix products  42.1 us (8%)
  other arithmetic  21.6 us (4%)
  starting transfers between devices  17.5 us (3%)
  between operations  15.4 us (3%)
    unnamed x7, waiting for transfers between devices  149 us
    reduce_scatter x1, waiting for transfers between devices, shards(): lax.psum_scatter(grad_qkv, 'tm', scatter_dimension=0, tiled=True)  70.7 us
    all_to_all x1, blocking collectives, shards(): lax.all_to_all(proj_grad_patches, 'tm', split_axis=0, concat_axis=1, tile...  56.7 us
    dot_general x11, matrix products, mixing(): return jnp.einsum(form, left, right, preferred_element_type=jnp.float32)  42.1 us
    all_gather x1, waiting for transfers between devices, shards(): lax.all_gather(w_qkv, 'tm', axis=0, tiled=True)  39.7 us
    all_gather x1, waiting for transfers between devices, shards(): lax.all_gather(w_out, 'tm', axis=0, tiled=True)  35.7 us
    all_to_all x1, waiting for transfers between devices, shards(): lax.all_to_all(projected, 'tm', split_axis=1, concat_axis=0, tiled=True)  26.4 us
    unnamed x41, local copies, waits for them, and re-layouts  13.1 us
  transfers between devices with their start and end apart: 8, of which 6 were waited for; matrix products, arithmetic and copies ran while one was open for 13% of the time, Pallas kernels for 0%

commit v1 on v0

v1 whole, which is shorter than its diff:
```python
import math

import jax
import jax.numpy as jnp
from jax import lax
from jax.experimental import pallas as pl
from jax.experimental.pallas import tpu as pltpu
from jax.sharding import PartitionSpec as P

F32, BF16 = jnp.float32, jnp.bfloat16
MESH = pl.DeviceIdType.MESH
HEADS, HEAD, PADDED = 8, 72, 80
EPS = 1e-6
D, FR, PATCH, LOCAL = 1152, 256, 48, 16
FACTOR = 1.0 / math.sqrt(HEAD)
EXP2 = FACTOR * math.log2(math.e)
OR = HEADS * PADDED
QR = 3 * OR
ROWS = 768
GRAD_SCALE = 1.0 / math.sqrt(16 * 256 * 48)
TILES = 18


def nn(a, b):
    return lax.dot_general(a, b, (((1,), (0,)), ((), ())), preferred_element_type=F32)


def nt(a, b):
    return lax.dot_general(a, b, (((1,), (1,)), ((), ())), preferred_element_type=F32)


def tn(a, b):
    return lax.dot_general(a, b, (((0,), (0,)), ((), ())), preferred_element_type=F32)


def grid2(shape):
    return lax.broadcasted_iota(jnp.int32, shape, 0), lax.broadcasted_iota(jnp.int32, shape, 1)


def padded(r):
    return lax.div(r, HEAD) * PADDED + lax.rem(r, HEAD)


def onehot(cond):
    return jnp.where(cond, 1.0, 0.0).astype(BF16)


def swap_matrix():
    r, c = grid2((256, 256))
    return onehot(c == lax.rem(r, 16) * 16 + lax.div(r, 16))


def prep_weights(wbuf, wc, wt):
    r, c = grid2((144, 160))
    sel = onehot(c == padded(r))
    for u in range(8):
        for i in range(TILES // 2):
            block = jnp.concatenate(
                [jnp.concatenate([wbuf[2 * i + k, core, u] for k in range(2)], axis=1) for core in range(2)], axis=0
            )
            wc[144 * u : 144 * u + 144, 256 * i : 256 * i + 256] = nn(sel, block).astype(BF16)
    r, c = grid2((160, 256))
    d = lax.rem(r, PADDED)
    target = lax.div(r, PADDED) * HEAD + d
    for j in range(16):
        lo = 128 * ((144 * j) // 128)
        e = onehot((d < HEAD) & (c == target + (144 * j - lo)))
        wt[160 * j : 160 * j + 160, :] = nt(e, wc[:, lo : lo + 256]).astype(BF16)


def head_step(h, p, pt, ot, dp, at):
    def rows(base):
        return pl.ds(pl.multiple_of(base + PADDED * h, 16), PADDED)

    cols = pl.ds(pl.multiple_of(p * FR, FR), FR)
    q, k, v, o = pt[rows(0), :], pt[rows(OR), :], pt[rows(2 * OR), :], ot[rows(0), :]
    s = tn(k, q)
    top = jnp.max(s, axis=0, keepdims=True)
    e = jnp.exp2((s - top) * EXP2)
    probs = e * (1.0 / jnp.sum(e, axis=0, keepdims=True))
    low = probs.astype(BF16)
    pg = tn(v, o)
    ds = (probs * (pg - jnp.sum(probs * pg, axis=0, keepdims=True))).astype(BF16)
    at[rows(0), cols] = nn(v, low).astype(BF16)
    dp[rows(0), cols] = (nn(k, ds) * FACTOR).astype(BF16)
    dp[rows(OR), cols] = (nt(q, ds) * FACTOR).astype(BF16)
    dp[rows(2 * OR), cols] = nt(o, low).astype(BF16)


def patch_step(p, x, g, scale, gate, wt, mod_ref, bg_ref, pt, ot, dp, at, unit_ref, out):
    rows = pl.ds(pl.multiple_of(p * FR, FR), FR)
    values = x[p].astype(F32)
    cen = values - jnp.mean(values, axis=-1, keepdims=True)
    inv = lax.rsqrt(jnp.mean(cen * cen, axis=-1, keepdims=True) + EPS)
    unit = cen * inv
    unit_ref[...] = unit
    mod = (unit * (1.0 + scale)).astype(BF16)
    mod_ref[rows, :] = mod
    pt[...] = nt(wt[0:QR, :], mod).astype(BF16)
    bg = (g[p].astype(F32) * gate).astype(BF16)
    bg_ref[rows, :] = bg
    ot[...] = nt(wt[QR : QR + OR, :], bg).astype(BF16)

    def body(h, carry):
        head_step(h, p, pt, ot, dp, at)
        return carry

    lax.fori_loop(0, HEADS, body, 0, unroll=True)
    ug = tn(dp[:, rows], wt[0:QR, :]) * (1.0 + scale)
    unit = unit_ref[...]
    branch = inv * (
        ug - jnp.mean(ug, axis=-1, keepdims=True) - unit * jnp.mean(ug * unit, axis=-1, keepdims=True)
    )
    out[p] = (g[p].astype(F32) + branch).astype(BF16)


def weight_grads(par, group, mod_ref, bg_ref, dp, at, l1, l2, dw):
    r, c = grid2((112, 160))
    sel1 = onehot((r < 108) & (c == padded(r + 36 * par)))
    r, c = grid2((48, 80))
    sel2 = onehot((r >= 12) & (c == r - 12 + 36 * par))
    for i in range(4):
        half = 4 * (i % 2) + 2 * group + i // 2
        lo = pl.multiple_of(240 * half + 80 * par, 16)
        l1[112 * i : 112 * i + 112, :] = nn(sel1, dp[pl.ds(lo, 160), :]).astype(BF16)
        l2[48 * i : 48 * i + 48, :] = nn(sel2, at[PADDED * half : PADDED * half + PADDED, :]).astype(BF16)
    t1 = nn(l1[...], mod_ref[...])
    t2 = nn(l2[...], bg_ref[...])
    for i in range(4):
        a, b = t1[112 * i : 112 * i + 112], t2[48 * i : 48 * i + 48]
        dw[4 * group + i, 0:96, :] = a[0:96].astype(BF16)
        dw[4 * group + i, 96:112, :] = (a[96:112] + b[0:16]).astype(BF16)
        dw[4 * group + i, 112:144, :] = b[16:48].astype(BF16)


def add(a, b):
    return (a.astype(F32) + b.astype(F32)).astype(BF16)


def wait_bytes(ref, sem):
    pltpu.make_async_copy(ref, ref, sem).wait()


def main_kernel(
    tok, dout, wsrc, scale_ref, gate_ref,
    back, dwq, dwo,
    tok_in, dout_in, tok_tx, dout_tx, x, g, wbuf, wc, wt, mod_ref, bg_ref, pt, ot, dp, at, unit_ref, l1, l2, dtok,
    dw_tx, dw_own, core_rx, up_rx, dn_rx, xh_rx, tm_tx, tm_rx,
    in_sem, w_send, w1_sem, up_sem, dn_sem, wcore_sem, a_send, x_sem, g_sem, back_send, back_sem,
    core_send, core_sem, up_send, dn_send, up_recv, dn_recv, xh_send, xh_sem, tm_send, tm_sem,
):
    tm, dpi = lax.axis_index("tm"), lax.axis_index("dp")
    xl, y, c = lax.div(tm, 8), lax.rem(lax.div(tm, 2), 4), lax.rem(tm, 2)
    xh, z = lax.div(dpi, 8), lax.rem(dpi, 8)
    mine8 = xl * 4 + y

    def peer(a, b, cc):
        return {"tm": lax.rem(xl + a, 2) * 8 + lax.rem(y + b, 4) * 2 + lax.rem(c + cc, 2), "dp": dpi}

    def ring(step):
        return {"tm": tm, "dp": xh * 8 + lax.rem(z + step + 8, 8)}

    partner = peer(0, 0, 1)
    across = {"tm": tm, "dp": lax.rem(dpi + 8, 16)}
    peers = [(a, b, cc) for a in range(2) for b in range(4) for cc in range(2) if (a, b, cc) != (0, 0, 0)]

    def send(src, dst, ssem, rsem, target):
        copy = pltpu.make_async_remote_copy(
            src_ref=src, dst_ref=dst, send_sem=ssem, recv_sem=rsem, device_id=target, device_id_type=MESH
        )
        copy.start()

    in0 = pltpu.make_async_copy(tok, tok_in, in_sem.at[0])
    in1 = pltpu.make_async_copy(dout, dout_in, in_sem.at[1])
    in0.start()
    in1.start()

    barrier = pltpu.get_barrier_semaphore()
    for target in [peer(*o) for o in peers] + [ring(1), ring(-1), across]:
        pl.semaphore_signal(barrier, inc=1, device_id=target, device_id_type=MESH)
    pl.semaphore_wait(barrier, 18)

    first, extra = pl.ds(2 * z, 2), 16 + z
    pltpu.make_async_copy(wsrc.at[first], wbuf.at[first, c, mine8], w1_sem.at[0]).start()
    for a in range(2):
        for b in range(4):
            if (a, b) != (0, 0):
                send(wsrc.at[first], wbuf.at[first, c, mine8], w_send.at[0], w1_sem.at[0], peer(a, b, 0))

    @pl.when(z < 2)
    def _():
        pltpu.make_async_copy(wsrc.at[extra], wbuf.at[extra, c, mine8], w1_sem.at[1]).start()
        for a in range(2):
            for b in range(4):
                if (a, b) != (0, 0):
                    send(wsrc.at[extra], wbuf.at[extra, c, mine8], w_send.at[1], w1_sem.at[1], peer(a, b, 0))

    swap = swap_matrix()
    for n, (src, tx) in enumerate(((tok_in, tok_tx), (dout_in, dout_tx))):
        (in0, in1)[n].wait()
        for b in range(3):
            block = src[:, 16 * b : 16 * b + 16, :].reshape(256, D)
            tx[16 * b : 16 * b + 16] = nn(swap, block).astype(BF16).reshape(16, 16, D)
    mine16 = pl.ds(pl.multiple_of(LOCAL * tm, LOCAL), LOCAL)
    for p in range(3):
        for tx, rx, sem in ((tok_tx, x, x_sem), (dout_tx, g, g_sem)):
            pltpu.make_async_copy(tx.at[3 * tm + p], rx.at[p, mine16], sem.at[p]).start()
            for o in peers:
                target = peer(*o)
                send(tx.at[3 * target["tm"] + p], rx.at[p, mine16], a_send.at[0], sem.at[p], target)

    def pmain(q):
        return wbuf.at[pl.ds(2 * q, 2), c]

    def ptile(q, k):
        return wbuf.at[2 * q + k, c]

    def pextra(q):
        return wbuf.at[16 + q, c]

    wait_bytes(pmain(z), w1_sem.at[0])
    send(pmain(z), pmain(z), w_send.at[2], up_sem.at[0, 0], ring(1))
    send(pmain(z), pmain(z), w_send.at[3], dn_sem.at[0, 0], ring(-1))
    send(pmain(z), pmain(z), w_send.at[4], wcore_sem.at[0], partner)

    @pl.when(z < 2)
    def _():
        wait_bytes(pextra(z), w1_sem.at[1])
        send(pextra(z), pextra(z), w_send.at[5], up_sem.at[0, 1], ring(1))
        send(pextra(z), pextra(z), w_send.at[6], dn_sem.at[0, 1], ring(-1))
        send(pextra(z), pextra(z), w_send.at[7], wcore_sem.at[1], partner)

    for k in range(1, 5):
        for sem, way in ((up_sem, 1), (dn_sem, -1)):
            q = lax.rem(z - way * k + 8, 8)
            if k < 4:
                wait_bytes(pmain(q), sem.at[k - 1, 0])
                if k < 3:
                    send(pmain(q), pmain(q), w_send.at[2 + (way < 0)], sem.at[k, 0], ring(way))
                else:
                    half = ptile(q, int(way < 0))
                    send(half, half, w_send.at[8 + (way < 0)], sem.at[k, 0], ring(way))
                send(pmain(q), pmain(q), w_send.at[4], wcore_sem.at[0], partner)

                @pl.when(q < 2)
                def _():
                    wait_bytes(pextra(q), sem.at[k - 1, 1])
                    if k < 3 or way > 0:
                        send(pextra(q), pextra(q), w_send.at[5 + (way < 0)], sem.at[k, 1], ring(way))
                    send(pextra(q), pextra(q), w_send.at[7], wcore_sem.at[1], partner)
            else:
                half = ptile(q, int(way < 0))
                wait_bytes(half, sem.at[3, 0])
                send(half, half, w_send.at[4], wcore_sem.at[0], partner)
                if way > 0:

                    @pl.when(q < 2)
                    def _():
                        wait_bytes(pextra(q), sem.at[3, 1])
                        send(pextra(q), pextra(q), w_send.at[7], wcore_sem.at[1], partner)

    wait_bytes(wbuf.at[pl.ds(0, 16), 1 - c], wcore_sem.at[0])
    wait_bytes(wbuf.at[pl.ds(16, 2), 1 - c], wcore_sem.at[1])
    prep_weights(wbuf, wc, wt)

    scale, gate = scale_ref[...], gate_ref[...]
    for p in range(3):
        wait_bytes(x.at[p], x_sem.at[p])
        wait_bytes(g.at[p], g_sem.at[p])
        patch_step(p, x, g, scale, gate, wt, mod_ref, bg_ref, pt, ot, dp, at, unit_ref, dtok)
        pltpu.make_async_copy(dtok.at[p, mine16], back.at[3 * tm + p], back_sem.at[0]).start()
        for o in peers:
            target = peer(*o)
            theirs = pl.ds(pl.multiple_of(LOCAL * target["tm"], LOCAL), LOCAL)
            send(dtok.at[p, theirs], back.at[3 * tm + p], back_send.at[0], back_sem.at[0], target)

    for group in range(2):
        weight_grads(1 - c, group, mod_ref, bg_ref, dp, at, l1, l2, dw_tx)
        part = pl.ds(4 * group, 4)
        send(dw_tx.at[part], core_rx.at[part], core_send.at[group], core_sem.at[group], partner)
    for group in range(2):
        weight_grads(c, group, mod_ref, bg_ref, dp, at, l1, l2, dw_own)
    for group in range(2):
        part = pl.ds(4 * group, 4)
        wait_bytes(core_rx.at[part], core_sem.at[group])
        for i in range(4 * group, 4 * group + 4):
            dw_own[i] = add(dw_own[i], core_rx[i])

    even = lax.rem(z + c, 2) == 0

    def unit(step):
        return lax.div(lax.rem(z + step + 8, 8), 2) * 2

    ways = ((1, up_rx, up_send, up_recv), (-1, dn_rx, dn_send, dn_recv))

    @pl.when(even)
    def _():
        for way, rx, ssem, rsem in ways:
            own = unit(4) + int(way < 0)
            send(dw_own.at[own], rx.at[0, int(way < 0)], ssem.at[0], rsem.at[0, int(way < 0)], ring(way))
        for i in range(2):
            for way, rx, ssem, rsem in ways:
                own = unit(2 * way) + i
                wait_bytes(rx.at[0, i], rsem.at[0, i])
                dw_own[own] = add(dw_own[own], rx[0, i])
                send(dw_own.at[own], rx.at[1, i], ssem.at[1 + i], rsem.at[1, i], ring(way))
        for i in range(2):
            own = unit(0) + i
            wait_bytes(up_rx.at[1, i], up_recv.at[1, i])
            wait_bytes(dn_rx.at[1, i], dn_recv.at[1, i])
            dw_own[own] = (
                dw_own[own].astype(F32) + up_rx[1, i].astype(F32) + dn_rx[1, i].astype(F32)
            ).astype(BF16)
        send(dw_own.at[unit(0) + 1 - xh], xh_rx, xh_send.at[0], xh_sem.at[0], across)
        wait_bytes(xh_rx, xh_sem.at[0])
        total = add(dw_own[unit(0) + xh], xh_rx[...])
        dw_own[unit(0) + xh] = total
        r, cl = grid2((80, 256))
        for t in range(16):
            lo = min(128 * ((72 * t) // 128), 896)
            sel = onehot((r < HEAD) & (cl == r + (72 * t - lo)))
            tm_tx[t, :, 0:144] = nt(sel, dw_own[unit(0) + xh, :, lo : lo + 256]).astype(BF16)
        pltpu.make_async_copy(tm_tx.at[tm], tm_rx.at[mine8], tm_sem.at[0]).start()
        for o in peers:
            target = peer(*o)
            send(tm_tx.at[target["tm"]], tm_rx.at[mine8], tm_send.at[0], tm_sem.at[0], target)
        for way, rx, ssem, rsem in ways:
            for n in range(3):
                wait_bytes(dw_own.at[0], ssem.at[n])
        wait_bytes(xh_rx, xh_send.at[0])
        wait_bytes(tm_tx.at[pl.ds(0, 15)], tm_send.at[0])

    @pl.when(jnp.logical_not(even))
    def _():
        for way, rx, ssem, rsem in ways:
            i = int(way < 0)
            own = unit(3 * way) + i
            wait_bytes(rx.at[0, i], rsem.at[0, i])
            dw_own[own] = add(dw_own[own], rx[0, i])
            send(dw_own.at[own], rx.at[0, i], ssem.at[0], rsem.at[0, i], ring(way))
        for way, rx, ssem, rsem in ways:
            i = int(way > 0)
            send(dw_own.at[unit(3 * way) + i], rx.at[0, i], ssem.at[1], rsem.at[0, i], ring(way))
        for i in range(2):
            for way, rx, ssem, rsem in ways:
                own = unit(way) + i
                wait_bytes(rx.at[1, i], rsem.at[1, i])
                dw_own[own] = add(dw_own[own], rx[1, i])
                send(dw_own.at[own], rx.at[1, i], ssem.at[2 + i], rsem.at[1, i], ring(way))
        for way, rx, ssem, rsem in ways:
            for n in range(4):
                wait_bytes(dw_own.at[0], ssem.at[n])

    wait_bytes(tm_rx, tm_sem.at[0])
    total = tm_rx[0].astype(F32)
    for i in range(1, 8):
        total = total + tm_rx[i].astype(F32)
    total = total * GRAD_SCALE
    dwq[...] = total[0:HEAD, 0:108]
    dwo[...] = total[0:HEAD, 108:144]

    wait_bytes(back, back_sem.at[0])
    wait_bytes(tok_tx.at[pl.ds(0, 45)], a_send.at[0])
    wait_bytes(tok_tx.at[pl.ds(0, 45)], a_send.at[0])
    wait_bytes(tok_tx.at[pl.ds(0, 45)], back_send.at[0])
    for group in range(2):
        wait_bytes(core_rx.at[pl.ds(0, 4)], core_send.at[group])
    wait_bytes(wbuf.at[pl.ds(0, 2), 0, pl.ds(0, 7)], w_send.at[0])
    for n in (2, 3):
        wait_bytes(wbuf.at[pl.ds(0, 6), 0], w_send.at[n])
    wait_bytes(wbuf.at[pl.ds(0, 16), 0], w_send.at[4])
    for n in (8, 9):
        wait_bytes(wbuf.at[0, 0], w_send.at[n])

    @pl.when(z < 2)
    def _():
        wait_bytes(wbuf.at[0, 0, pl.ds(0, 7)], w_send.at[1])

    for n, steps in ((5, (0, -1, -2, -3)), (6, (0, 1, 2))):
        for s in steps:
            @pl.when(lax.rem(z + s + 8, 8) < 2)
            def _():
                wait_bytes(wbuf.at[0, 0], w_send.at[n])
    wait_bytes(wbuf.at[pl.ds(0, 2), 0], w_send.at[7])


def main_call(tok, dout, wsrc, scale, gate):
    vmem, anyspace = pl.BlockSpec(memory_space=pltpu.VMEM), pl.BlockSpec(memory_space=pl.ANY)
    dma = pltpu.SemaphoreType.DMA
    rows3 = pltpu.VMEM((3, FR, D), BF16)
    sent = pltpu.VMEM((PATCH, LOCAL, D), BF16)
    chunks = pltpu.VMEM((8, 144, D), BF16)
    passed = pltpu.VMEM((2, 2, 144, D), BF16)
    return pl.pallas_call(
        main_kernel,
        out_shape=(
            jax.ShapeDtypeStruct((PATCH, LOCAL, D), BF16),
            jax.ShapeDtypeStruct((HEAD, 108), F32),
            jax.ShapeDtypeStruct((HEAD, 36), F32),
        ),
        in_specs=[anyspace, anyspace, anyspace, vmem, vmem],
        out_specs=(anyspace, vmem, vmem),
        scratch_shapes=[
            pltpu.VMEM((LOCAL, PATCH, D), BF16), pltpu.VMEM((LOCAL, PATCH, D), BF16), sent, sent, rows3, rows3,
            pltpu.VMEM((TILES, 2, 8, PADDED, 128), BF16), pltpu.VMEM((D, 128 * TILES), BF16),
            pltpu.VMEM((QR + OR, D), BF16), pltpu.VMEM((ROWS, D), BF16), pltpu.VMEM((ROWS, D), BF16),
            pltpu.VMEM((QR, FR), BF16), pltpu.VMEM((OR, FR), BF16),
            pltpu.VMEM((QR, ROWS), BF16), pltpu.VMEM((OR, ROWS), BF16), pltpu.VMEM((FR, D), F32),
            pltpu.VMEM((448, ROWS), BF16), pltpu.VMEM((192, ROWS), BF16), rows3,
            chunks, chunks, chunks, passed, passed, pltpu.VMEM((144, D), BF16),
            pltpu.VMEM((16, 80, 256), BF16), pltpu.VMEM((8, 80, 256), BF16),
            dma((2,)), dma((10,)), dma((2,)), dma((4, 2)), dma((4, 2)), dma((2,)), dma((1,)), dma((3,)), dma((3,)),
            dma((1,)), dma((1,)),
            dma((2,)), dma((2,)), dma((4,)), dma((4,)), dma((2, 2)), dma((2, 2)), dma((1,)), dma((1,)), dma((1,)),
            dma((1,)),
        ],
        compiler_params=pltpu.CompilerParams(
            collective_id=0, has_side_effects=True, vmem_limit_bytes=62 << 20
        ),
        name="main",
    )(tok, dout, wsrc, scale, gate)


def unswap_kernel(src, dst):
    block = src[...].reshape(256, D)
    dst[...] = nn(swap_matrix(), block).astype(BF16).reshape(LOCAL, 16, D)


def unswap(back):
    return pl.pallas_call(
        unswap_kernel,
        grid=(3,),
        out_shape=jax.ShapeDtypeStruct((LOCAL, PATCH, D), BF16),
        in_specs=[pl.BlockSpec((16, LOCAL, D), lambda i: (i, 0, 0))],
        out_specs=pl.BlockSpec((LOCAL, 16, D), lambda i: (0, i, 0)),
        compiler_params=pltpu.CompilerParams(vmem_limit_bytes=16 << 20),
        name="unswap",
    )(back)


def shards(tokens, mod_scale, mod_gate, w_qkv, w_out, d_out):
    w = jnp.concatenate([w_qkv, w_out], axis=1)
    w = jnp.pad(w, ((0, PADDED - HEAD), (0, 0))).reshape(PADDED, TILES, 128).transpose(1, 0, 2)
    back, dwq, dwo = main_call(tokens[0], d_out[0], w, mod_scale, mod_gate)
    return unswap(back)[None], dwq, dwo


def solution(mesh):
    return jax.shard_map(
        shards,
        mesh=mesh,
        in_specs=(
            P("dp", "tm", None, None),
            P("dp", None),
            P("dp", None),
            P("tm", None),
            P("tm", None),
            P("dp", "tm", None, None),
        ),
        out_specs=(P("dp", "tm", None, None), P("tm", "dp"), P("tm", "dp")),
        check_vma=False,
    )
```

time: 541 us -> 152 us (0.28); the launches traced: 530 us -> 149 us
  waiting for transfers between devices: 330 us -> 0 us
  Pallas kernels: 0 us -> 144 us
  blocking collectives: 56.7 us -> 0 us
  local copies, waits for them, and re-layouts: 46.7 us -> 2.78 us
  matrix products: 42.1 us -> 0 us
  other arithmetic: 21.6 us -> 1.83 us
  starting transfers between devices: 17.5 us -> 0 us
  between operations: 15.4 us -> 0.88 us
    unnamed x7 -> x0, waiting for transfers between devices: 149 us -> none
    pallas_call x0 -> x2, Pallas kernels: none -> 144 us  [the longest x1 141 us: main_call(): pl.pallas_call(main_kernel, out_shape=(jax.ShapeDtypeStruct((PATCH, LOCAL...]
    all_gather x2 -> x0, waiting for transfers between devices: 75.4 us -> none  [the longest x1 39.7 us: shards(): lax.all_gather(w_qkv, 'tm', axis=0, tiled=True)]
    reduce_scatter x1 -> x0, waiting for transfers between devices: 70.7 us -> none  [shards(): lax.psum_scatter(grad_qkv, 'tm', scatter_dimension=0, tiled=True)]
    all_to_all x1 -> x0, blocking collectives: 56.7 us -> none  [shards(): lax.all_to_all(proj_grad_patches, 'tm', split_axis=0, concat_axis=1, tile...]
    dot_general x11 -> x0, matrix products: 42.1 us -> none  [mixing(): return jnp.einsum(form, left, right, preferred_element_type=jnp.float32)]
    all_to_all x3 -> x0, waiting for transfers between devices: 34.8 us -> none  [the longest x1 26.4 us: shards(): lax.all_to_all(projected, 'tm', split_axis=1, concat_axis=0, tiled=True)]
    reshape x5 -> x0, local copies, waits for them, and re-layouts: 19.8 us -> none  [the longest x2 6.56 us: attention_grads(): grad_view = attn_grad.reshape(frames, patches, head_count, head_dim)]
  transfers between devices with their start and end apart: 8 -> 0, of which waited for: 6 -> 0; matrix products, arithmetic and copies ran while one was open for 13% -> 0% of each run, Pallas kernels for 0% -> 0%
where the time goes in v1:
time: 152 us; the launch traced here: 149 us
  Pallas kernels  144 us (95%)
  local copies, waits for them, and re-layouts  2.78 us (2%)
  other arithmetic  1.83 us (1%)
    pallas_call x1, Pallas kernels, main_call(): pl.pallas_call(main_kernel, out_shape=(jax.ShapeDtypeStruct((PATCH, LOCAL...  141 us

profile of v1, /device:TPU:1, one launch (start us, length us, event | category | flops | bytes accessed | tf_op | source)
XLA Modules:
  0.0 149.0 jit_solution(1772994119389276091)
XLA Ops:
  0.6 1.8 %bitcast_bitcast_fusion.wsrc = bf16[18,80,128]{2,1,0:T(8,128)(2,1)} fusion(bf16[72,576]{1,0:T(8,128)(2,1)} %param.10, bf16[72,1728]{1,0:T(8,128)(2,1)} %param.9), kind=kLoop, calls=%fused_computation.5 | loop fusion | flops 1290240 | bytes 700416 | tf_op jit(solution)/shard_map/transpose | solution.py:443
  2.5 141.2 %main.1 = (bf16[48,16,1152]{2,1,0:T(8,128)(2,1)}, f32[72,108]{1,0:T(8,128)}, f32[72,36]{1,0:T(8,128)}) custom-call(bf16[16,48,1152]{2,1,0:T(8,128)(2,1)} %bitcast.10, bf16[16,48,1152]{2,1,0:T(8,128)(2,1)} %bitcast.11, bf16[18,80,128]{2,1,0:T(8,128)(2,1)} %bitcast_bitcast_fusion.wsrc, f32[1,1152]{1,0:T(1,128)} %scale_ref.1, f32[1,1152]{1,0:T(1,128)} %gate_ref.1), custom_call_target="tpu_custom_call" | custom-call | tf_op jit(solution)/shard_map/main/pallas_call | solution.py:394
  143.7 0.0 copy-start
  143.7 1.5 copy-done
  145.1 0.0 copy-start.2
  145.1 0.0 copy-start.1
  145.1 2.3 %unswap.1 = bf16[16,48,1152]{2,1,0:T(8,128)(2,1)} custom-call(bf16[48,16,1152]{2,1,0:T(8,128)(2,1)S(1)} %copy-done), custom_call_target="tpu_custom_call" | custom-call | tf_op jit(solution)/shard_map/unswap/pallas_call | solution.py:430
  147.5 0.0 copy-done.2
  147.5 0.7 copy.11
  148.2 0.0 copy-done.1
  148.2 0.6 copy.15
Async XLA Ops:
  143.7 1.5 copy-start
  145.1 2.3 %copy-start.2 = (f32[72,36]{1,0:T(8,128)S(1)}, f32[72,36]{1,0:T(8,128)}, u32[]{:S(2)}) copy-start(f32[72,36]{1,0:T(8,128)} %get-tuple-element.14) | copy-start | bytes 31108
  145.1 3.0 %copy-start.1 = (f32[72,108]{1,0:T(8,128)S(1)}, f32[72,108]{1,0:T(8,128)}, u32[]{:S(2)}) copy-start(f32[72,108]{1,0:T(8,128)} %get-tuple-element.19) | copy-start | bytes 93316
